TPU v7x, 256 devices: a whole 4x4x8 slice. The times are simulated.
256 devices in a mesh: grp: 8 (over z_hi, x), wk: 32 (over z_lo, y, core).
Axes of the slice: x: 4, y: 4, z: 8 (z_hi: 2, z_lo: 4; z = z_hi * 4 + z_lo), core: 2. Of those that a mesh axis runs over, the one named last changes fastest.
Arguments:
- grads: bfloat16 [8, 4, 512, 1024], P('grp', None, 'wk'), may hold values from -4 to 4
- bank: bfloat16 [32, 5, 512, 512], P('wk'), as said below
- owners: int32 [4], replicated, may hold values from 0 to 31, as said below
- col_map: int32 [4, 2], replicated, may hold values from 0 to 3
Outputs:
- update: float32 [4, 512, 1024], P(None, 'grp', 'wk')
Inputs may be any that keep to these rules, and one draw needn't show every extreme that they name: `owners`: 4 distinct worker indices; the last worker serves one of the layers. `bank`: every block is symmetric.
All inputs are finite; a program needn't handle non-finite values.
Results may differ from a plain program's by a relative error of at most 0.015.
Values may be sent and summed in bfloat16 or wider, within the bound.
A program may use at most 64 MiB of HBM per device.

v0:
```python
import jax
import jax.numpy as jnp
from jax import lax
from jax.sharding import PartitionSpec as P


def spread(value, axis, root):
    mine = lax.axis_index(axis) == root
    return lax.psum(jnp.where(mine, value, jnp.zeros_like(value)), axis)


def right_multiply(rows_in, right_blocks):
    rows_count = rows_in.shape[0]
    blocks = right_blocks.shape[0]
    block = right_blocks.shape[1]
    split_rows = rows_in.reshape(rows_count, blocks, block)
    mixed = jnp.einsum("nkb,kbc->nkc", split_rows, right_blocks, preferred_element_type=jnp.float32)
    return mixed.reshape(rows_count, blocks * block).astype(jnp.bfloat16)


def on_device(grads, bank, owners, col_map):
    layer_total = grads.shape[1]
    width_total = grads.shape[3]
    block = bank.shape[2]
    rows_output = block // lax.axis_size("grp")
    row_offset = lax.axis_index("grp") * rows_output
    col_count = width_total // lax.axis_size("wk")
    col_offset = lax.axis_index("wk") * col_count
    results = []
    for layer_index in range(layer_total):
        chosen = jnp.take(bank[0, 1:], col_map[layer_index], axis=0)
        selected = jnp.concatenate([bank[0, :1], chosen], axis=0)
        factors = spread(selected, "wk", owners[layer_index])
        left_inverse = factors[0]
        right_blocks = factors[1:]
        left_rows = lax.dynamic_slice_in_dim(left_inverse, row_offset, rows_output, 0)
        summed = lax.psum(grads[0, layer_index].astype(jnp.float32).astype(jnp.bfloat16), "grp")
        mixed_full = right_multiply(lax.all_gather(summed, "wk", axis=0, tiled=True), right_blocks)
        mixed_cols = lax.dynamic_slice_in_dim(mixed_full, col_offset, col_count, 1)
        output_rows = jnp.dot(left_rows, mixed_cols, preferred_element_type=jnp.float32)
        results.append(output_rows)
    return jnp.stack(results)


def solution(mesh):
    in_specs = (P("grp", None, "wk", None), P("wk", None, None, None), P(), P())
    out_specs = P(None, "grp", "wk")
    return jax.shard_map(
        on_device, mesh=mesh, in_specs=in_specs, out_specs=out_specs, check_vma=False
    )
```

profile of v0, /device:TPU:1, one launch (start us, length us, event | category | flops | bytes accessed | tf_op | source)
XLA Modules:
  0.0 668.4 jit_solution(14254915636885988348)
XLA Ops:
  6.5 1.5 slice_bitcast_fusion.4
  8.1 106.8 %all-reduce.7.cloned.1.call-done = (bf16[16,1024]{1,0:T(8,128)(2,1)}, bf16[16,1024]{1,0:T(8,128)(2,1)}, bf16[16,1024]{1,0:T(8,128)(2,1)}, bf16[16,1024]{1,0:T(8,128)(2,1)}) async-done(((bf16[16,1024]{1,0:T(8,128)(2,1)}, bf16[16,1024]{1,0:T(8,128)(2,1)}, bf16[16,1024]{1,0:T(8,128)(2,1)}, bf16[16,1024]{1,0:T(8,128)(2,1)}), (bf16[16,1024]{1,0:T(8,128)(2,1)}, bf16[16,1024]{1,0:T(8,128)(2,1)}, ...) | async-done | bytes 131088 | tf_op jit(solution)/shard_map/psum | solution.py:37
  114.9 0.7 all-gather.7.cloned.1.call-update
  116.2 1.0 slice_reduce_fusion.3
  117.4 1.7 slice_bitcast_fusion
  119.2 1.9 slice.73
  121.1 1.6 gather_fusion.3
  122.7 1.5 copy.29
  124.2 1.6 gather_fusion.2
  125.7 2.3 copy.26
  128.0 1.6 gather_fusion.1
  129.6 2.3 copy.23
  131.9 1.6 gather_fusion
  133.5 1.5 copy.20
  138.2 2.1 copy.36
  140.7 1.0 copy-done.1
  142.1 0.9 copy-done.2
  142.9 2.9 fusion
  145.9 31.1 %all-gather.5.cloned.1.call-done = bf16[512,1024]{1,0:T(8,128)(2,1)} async-done(((bf16[16,1024]{1,0:T(8,128)(2,1)}), bf16[512,1024]{1,0:T(8,128)(2,1)}) %all-gather.5.cloned.1.call-update) | async-done | bytes 1048592 | tf_op jit(solution)/shard_map/all_gather | solution.py:38
  177.0 1.5 copy.21
  178.5 58.4 %all-gather.7.cloned.1.call-done = bf16[512,1024]{1,0:T(8,128)(2,1)} async-done(((bf16[16,1024]{1,0:T(8,128)(2,1)}), bf16[512,1024]{1,0:T(8,128)(2,1)}) %all-gather.7.cloned.1.call-update) | async-done | bytes 1048592 | tf_op jit(solution)/shard_map/all_gather | solution.py:38
  236.9 1.5 copy.24
  238.4 58.2 %all-gather.9.cloned.1.call-done = bf16[512,1024]{1,0:T(8,128)(2,1)} async-done(((bf16[16,1024]{1,0:T(8,128)(2,1)}), bf16[512,1024]{1,0:T(8,128)(2,1)}) %all-gather.9.cloned.1.call-update) | async-done | bytes 1048592 | tf_op jit(solution)/shard_map/all_gather | solution.py:38
  296.6 1.5 copy.27
  298.1 58.2 %all-gather.11.cloned.1.call-done = bf16[512,1024]{1,0:T(8,128)(2,1)} async-done(((bf16[16,1024]{1,0:T(8,128)(2,1)}), bf16[512,1024]{1,0:T(8,128)(2,1)}) %all-gather.11.cloned.1.call-update) | async-done | bytes 1048592 | tf_op jit(solution)/shard_map/all_gather | solution.py:38
  356.2 2.3 copy.30
  358.5 294.4 %all-reduce.5.cloned.1.call-done = (bf16[3,512,512]{1,2,0:T(8,128)(2,1)}, bf16[3,512,512]{1,2,0:T(8,128)(2,1)}, bf16[3,512,512]{1,2,0:T(8,128)(2,1)}, bf16[3,512,512]{1,2,0:T(8,128)(2,1)}) async-done(((bf16[3,512,512]{1,2,0:T(8,128)(2,1)}, bf16[3,512,512]{1,2,0:T(8,128)(2,1)}, bf16[3,512,512]{1,2,0:T(8,128)(2,1)}, bf16[3,512,512]{1,2,0:T(8,128)(2,1)}), (bf16[3,512,512]{1,2,0:T(8,128)(2,1)}, ...) | async-done | bytes 6291472 | tf_op jit(solution)/shard_map/psum | solution.py:9
  652.9 1.1 slice.102
  654.0 2.0 convolution_convert_fusion.3
  656.1 0.7 convolution_convert_fusion.2
  657.6 0.7 convolution_convert_fusion.1
  659.3 0.7 convolution_convert_fusion
  (46 shorter events, 5.4 us)
Async XLA Ops:
  6.5 108.3 %all-reduce.7.cloned.1.call-start = ((), (), s32[]{:S(2)}) async-start(), calls=%async_computation.5 | async-start | bytes 262144 | tf_op jit(solution)/shard_map/psum | solution.py:37
  8.0 169.0 %all-gather.5.cloned.1.call-start = ((), (), s32[]{:S(2)}) async-start(), calls=%async_computation | async-start | bytes 1081344 | tf_op jit(solution)/shard_map/all_gather | solution.py:38
  114.9 122.0 %all-gather.7.cloned.1.call-start = ((), (), s32[]{:S(2)}) async-start(), calls=%async_computation.1 | async-start | bytes 1081344 | tf_op jit(solution)/shard_map/all_gather | solution.py:38
  115.6 180.9 %all-gather.9.cloned.1.call-start = ((), (), s32[]{:S(2)}) async-start(), calls=%async_computation.2 | async-start | bytes 1081344 | tf_op jit(solution)/shard_map/all_gather | solution.py:38
  116.2 240.0 %all-gather.11.cloned.1.call-start = ((), (), s32[]{:S(2)}) async-start(), calls=%async_computation.3 | async-start | bytes 1081344 | tf_op jit(solution)/shard_map/all_gather | solution.py:38
  119.1 533.8 %all-reduce.5.cloned.1.call-start = ((), (), s32[]{:S(2)}) async-start(), calls=%async_computation.4 | async-start | bytes 12582912 | tf_op jit(solution)/shard_map/psum | solution.py:9
  133.5 1.5 copy-start.7
  138.2 2.4 copy-start
  140.5 1.2 copy-start.1
  141.9 1.0 copy-start.2
  654.0 2.1 copy-start.6
  656.1 1.4 copy-start.5
  657.6 1.4 copy-start.4
  657.6 1.7 copy-start.3
Sparse Core Ops, SparseCore 0:
  10.2 104.6 all-reduce.6
  116.9 60.0 all-gather.4
  179.0 57.8 all-gather.6
  238.7 57.7 all-gather.8
  298.4 57.7 all-gather.10
  359.2 293.6 all-reduce.4
where the time goes:
time: 669 us; the launch traced here: 668 us
  waiting for transfers between devices  608 us (91%)
  local copies, waits for them, and re-layouts  34.3 us (5%)
  between operations  16.2 us (2%)
    psum x1, waiting for transfers between devices, spread(): return lax.psum(jnp.where(mine, value, jnp.zeros_like(value)), axis)  294 us
    all_gather x4, waiting for transfers between devices, on_device(): lax.all_gather(summed, 'wk', axis=0, tiled=True)  206 us
    psum x1, waiting for transfers between devices, on_device(): lax.psum(grads[0, layer_index].astype(jnp.float32).astype(jnp.bfloat16),...  107 us
    gather x8, local copies, waits for them, and re-layouts, on_device(): chosen = jnp.take(bank[0, 1:], col_map[layer_index], axis=0)  14 us
  transfers between devices with their start and end apart: 6, of which 6 were waited for; matrix products, arithmetic and copies ran while one was open for 5% of the time, Pallas kernels for 0%

commit v1 on v0

v1 whole, which is shorter than its diff:
```python
import functools

import jax
import jax.numpy as jnp
from jax import lax
from jax.experimental import pallas as pl
from jax.experimental.pallas import tpu as pltpu
from jax.sharding import PartitionSpec as P

MESH = pl.DeviceIdType.MESH
NZ, NY, NC = 4, 4, 2
NG = 8
B = 512


def kernel(
    owners_ref, cmap_ref, grads_ref, bank_ref, out_ref,
    rx1, s_buf, l_buf, r_all, r_buf, r_tx, u_buf, rx3, p_buf, rx4,
    loc_sem, s1, r1, sz, rz, sy, ry, sc, rc, sf, rf, s3, r3, s4, r4,
):
    g = lax.axis_index("grp")
    w = lax.axis_index("wk")
    z, y, c = w // 8, (w // 2) % 4, w % 2
    l, j = g // 2, g % 2

    def wk(zz, yy, cc):
        return zz * 8 + yy * 2 + cc

    peer = (g, wk(z, y, 1 - c))

    def local(src, dst, sem):
        return pltpu.make_async_copy(src, dst, sem)

    def remote(src, dst, ssem, rsem, dev):
        return pltpu.make_async_remote_copy(
            src_ref=src, dst_ref=dst, send_sem=ssem, recv_sem=rsem,
            device_id=dev, device_id_type=MESH,
        )

    def grad_piece(g2):
        return grads_ref.at[g2 // 2, :, pl.ds(pl.multiple_of((g2 % 2) * B, B), B)]

    cp_g = local(grad_piece(g), rx1.at[NG - 1], loc_sem.at[0])
    cp_l = local(bank_ref.at[0], l_buf.at[c], loc_sem.at[1])
    cp_r = local(bank_ref.at[pl.ds(1, 4)], r_all, loc_sem.at[2])
    cp_g.start()
    cp_l.start()
    cp_r.start()

    barrier = pltpu.get_barrier_semaphore()
    count = 0
    for off in range(NG):
        for zo in range(NZ):
            if off or zo:
                pl.semaphore_signal(
                    barrier, inc=1, device_id=((g + off) % NG, wk((z + zo) % NZ, y, c)), device_id_type=MESH)
                count += 1
    for yo in range(1, NY):
        pl.semaphore_signal(barrier, inc=1, device_id=(g, wk(z, (y + yo) % NY, c)), device_id_type=MESH)
        count += 1
    pl.semaphore_signal(barrier, inc=1, device_id=peer, device_id_type=MESH)
    count += 1
    pl.semaphore_wait(barrier, count)

    sends = []
    first = []
    for off in range(1, NG):
        g2 = (g + off) % NG
        cp = remote(grad_piece(g2), rx1.at[off - 1], s1.at[off - 1], r1.at[off - 1], (g2, w))
        cp.start()
        first.append(cp)
    sends += first

    cp_l.wait()
    f_l = remote(l_buf.at[c], l_buf.at[c], sf.at[0], rf.at[0], peer)
    f_l.start()
    cp_r.wait()
    block = cmap_ref[l, j]
    for zz in range(2):
        for yy in range(NY):
            r_tx[yy, zz] = r_all[block, zz, yy, 1 - c]
    f_r = remote(r_tx, r_buf.at[c], sf.at[1], rf.at[1], peer)
    f_r.start()
    for zz in range(2):
        for yy in range(NY):
            r_buf[c, yy, zz] = r_all[block, zz, yy, c]
    sends += [f_l, f_r]

    cp_g.wait()
    for cp in first:
        cp.wait_recv()
    total = rx1[0].astype(jnp.float32)
    for k in range(1, NG):
        total += rx1[k].astype(jnp.float32)
    s_buf[z, y, c] = total.astype(jnp.bfloat16)

    zs = []
    for off in range(1, NZ):
        cp = remote(s_buf.at[z, y, c], s_buf.at[z, y, c], sz.at[off - 1], rz.at[off - 1],
                    (g, wk((z + off) % NZ, y, c)))
        cp.start()
        zs.append(cp)
    for cp in zs:
        cp.wait_recv()
    ys = []
    for off in range(1, NY):
        cp = remote(s_buf.at[:, y, c], s_buf.at[:, y, c], sy.at[off - 1], ry.at[off - 1],
                    (g, wk(z, (y + off) % NY, c)))
        cp.start()
        ys.append(cp)
    cs = []
    for off in range(NY):
        if off:
            ys[off - 1].wait_recv()
        yy = (y - off + NY) % NY
        cp = remote(s_buf.at[:, yy, c], s_buf.at[:, yy, c], sc.at[off], rc.at[off], peer)
        cp.start()
        cs.append(cp)
    sends += zs + ys + cs
    f_l.wait_recv()
    f_r.wait_recv()
    for cp in cs:
        cp.wait_recv()

    owner = owners_ref[l]
    o_y, o_c = (owner // 2) % 4, owner % 2
    right = r_buf[o_c].reshape(2 * NY * 32, B)
    summed = s_buf[...].reshape(B, B)
    mixed = lax.dot_general(right, summed, (((1,), (1,)), ((), ())), preferred_element_type=jnp.float32)
    update = jnp.dot(mixed.astype(jnp.bfloat16), l_buf[o_c].reshape(B, B), preferred_element_type=jnp.float32)
    u_buf[...] = update.astype(jnp.bfloat16).reshape(NY, 2, 32, B)

    us = []
    for off in range(1, NY):
        y2 = (y + off) % NY
        cp = remote(u_buf.at[y2], rx3.at[y], s3.at[off - 1], r3.at[off - 1], (g, wk(z, y2, c)))
        cp.start()
        us.append(cp)
    rx3[y] = u_buf[y]
    for cp in us:
        cp.wait_recv()
    sends += us

    low = lax.broadcasted_iota(jnp.int32, (16, 128), 1) < 64
    for zz in range(2):
        for b in range(4):
            top = rx3[o_y, zz, pl.ds(0, 16), pl.ds(128 * b, 128)].astype(jnp.float32)
            bot = rx3[o_y, zz, pl.ds(16, 16), pl.ds(128 * b, 128)].astype(jnp.float32)
            p_buf[zz, 2 * b] = jnp.where(low, top, pltpu.roll(bot, 64, 1)).astype(jnp.bfloat16)
            p_buf[zz, 2 * b + 1] = jnp.where(low, pltpu.roll(top, 64, 1), bot).astype(jnp.bfloat16)
    pending = []
    for zz in range(2):
        z2 = 2 * j + zz
        for off in range(NG):
            g2 = (g + off) % NG
            cp = remote(p_buf.at[zz, g2], rx4.at[l, z], s4.at[zz, off], r4.at[l, z], (g2, wk(z2, y, c)))
            if off:
                cp.start()
                sends.append(cp)
            else:
                own = local(p_buf.at[zz, g2], rx4.at[l, z], r4.at[l, z])

                pl.when(z2 == z)(own.start)
                pl.when(z2 != z)(cp.start)

                pending.append((z2, cp))
    for layer in range(4):
        for zz in range(NZ):
            local(p_buf.at[0, 0], rx4.at[layer, zz], r4.at[layer, zz]).wait()
    for z2, cp in pending:
        pl.when(z2 != z)(cp.wait_send)
    for cp in sends:
        cp.wait_send()
    for layer in range(4):
        out_ref[layer] = rx4[layer, owners_ref[layer] // 8].astype(jnp.float32)


def solution(mesh):
    def step(grads, bank, owners, cmap):
        packed = pl.pallas_call(
            kernel,
            out_shape=jax.ShapeDtypeStruct((4, 16, 128), jnp.float32),
            in_specs=[
                pl.BlockSpec(memory_space=pltpu.SMEM),
                pl.BlockSpec(memory_space=pltpu.SMEM),
                pl.BlockSpec(memory_space=pl.ANY),
                pl.BlockSpec(memory_space=pl.ANY),
            ],
            out_specs=pl.BlockSpec(memory_space=pltpu.VMEM),
            scratch_shapes=[
                pltpu.VMEM((NG, 16, B), jnp.bfloat16),
                pltpu.VMEM((NZ, NY, NC, 16, B), jnp.bfloat16),
                pltpu.VMEM((NC, 2, NY, NC, 32, B), jnp.bfloat16),
                pltpu.VMEM((4, 2, NY, NC, 32, B), jnp.bfloat16),
                pltpu.VMEM((NC, NY, 2, 32, B), jnp.bfloat16),
                pltpu.VMEM((NY, 2, 32, B), jnp.bfloat16),
                pltpu.VMEM((NY, 2, 32, B), jnp.bfloat16),
                pltpu.VMEM((NY, 2, 32, B), jnp.bfloat16),
                pltpu.VMEM((2, NG, 16, 128), jnp.bfloat16),
                pltpu.VMEM((4, NZ, 16, 128), jnp.bfloat16),
                pltpu.SemaphoreType.DMA((3,)),
                pltpu.SemaphoreType.DMA((NG - 1,)),
                pltpu.SemaphoreType.DMA((NG - 1,)),
                pltpu.SemaphoreType.DMA((NZ - 1,)),
                pltpu.SemaphoreType.DMA((NZ - 1,)),
                pltpu.SemaphoreType.DMA((NY - 1,)),
                pltpu.SemaphoreType.DMA((NY - 1,)),
                pltpu.SemaphoreType.DMA((NY,)),
                pltpu.SemaphoreType.DMA((NY,)),
                pltpu.SemaphoreType.DMA((2,)),
                pltpu.SemaphoreType.DMA((2,)),
                pltpu.SemaphoreType.DMA((NY - 1,)),
                pltpu.SemaphoreType.DMA((NY - 1,)),
                pltpu.SemaphoreType.DMA((2, NG)),
                pltpu.SemaphoreType.DMA((4, NZ)),
            ],
            compiler_params=pltpu.CompilerParams(
                collective_id=0, has_side_effects=True, vmem_limit_bytes=32 * 1024 * 1024
            ),
        )(owners, cmap, grads[0], bank.reshape(5, 2, NY, NC, 32, B))
        packed = packed.reshape(4, 16, 2, 64)
        return packed.transpose(0, 3, 2, 1).reshape(4, 64, 32)

    return jax.shard_map(
        step, mesh=mesh,
        in_specs=(P("grp", None, "wk", None), P("wk", None, None, None), P(), P()),
        out_specs=P(None, "grp", "wk"), check_vma=False,
    )
```

time: 669 us -> 45 us (0.07)
  waiting for transfers between devices: 608 us -> 0 us
  Pallas kernels: 0 us -> 40.1 us
  local copies, waits for them, and re-layouts: 34.3 us -> 4.79 us
  between operations: 16.2 us -> 0.02 us
    psum x2 -> x0, waiting for transfers between devices: 401 us -> none  [the longest x1 294 us: spread(): return lax.psum(jnp.where(mine, value, jnp.zeros_like(value)), axis)]
    all_gather x4 -> x0, waiting for transfers between devices: 206 us -> none  [on_device(): lax.all_gather(summed, 'wk', axis=0, tiled=True)]
    pallas_call x0 -> x1, Pallas kernels: none -> 40.1 us  [step(): pl.pallas_call(kernel, out_shape=jax.ShapeDtypeStruct((4, 16, 128), jnp.f...]
    gather x8 -> x0, local copies, waits for them, and re-layouts: 14 us -> none  [on_device(): chosen = jnp.take(bank[0, 1:], col_map[layer_index], axis=0)]
    all_gather x4 -> x0, local copies, waits for them, and re-layouts: 6.77 us -> none  [on_device(): lax.all_gather(summed, 'wk', axis=0, tiled=True)]
  transfers between devices with their start and end apart: 6 -> 0, of which waited for: 6 -> 0; matrix products, arithmetic and copies ran while one was open for 5% -> 0% of each run, Pallas kernels for 0% -> 0%
where the time goes in v1:
time: 45 us; the launch traced here: 44.9 us
  Pallas kernels  40.1 us (89%)
  local copies, waits for them, and re-layouts  4.79 us (11%)
    pallas_call x1, Pallas kernels, step(): pl.pallas_call(kernel, out_shape=jax.ShapeDtypeStruct((4, 16, 128), jnp.f...  40.1 us
    unnamed x7, local copies, waits for them, and re-layouts  4.06 us

profile of v1, /device:TPU:1, one launch (start us, length us, event | category | flops | bytes accessed | tf_op | source)
XLA Modules:
  0.0 44.9 jit_solution(11355899015149670898)
XLA Ops:
  0.0 0.8 %copy.5.cmap_ref = s32[4,2]{1,0:T(4,128)S(1)} copy(s32[4,2]{0,1:T(2,128)} %param.7) | data formatting | bytes 64 | tf_op args[3]
  0.8 0.0 copy-start
  0.8 1.7 %copy-done = bf16[1,5,512,512]{3,2,1,0:T(8,128)(2,1)S(1)} copy-done((bf16[1,5,512,512]{3,2,1,0:T(8,128)(2,1)S(1)}, bf16[1,5,512,512]{3,2,1,0:T(8,128)(2,1)}, u32[]{:S(2)}) %copy-start) | copy-done | bytes 2621464
  2.5 0.0 copy-start.1
  2.5 0.9 %copy-done.1 = bf16[1,4,16,1024]{3,2,1,0:T(8,128)(2,1)S(1)} copy-done((bf16[1,4,16,1024]{3,2,1,0:T(8,128)(2,1)S(1)}, bf16[1,4,16,1024]{3,2,1,0:T(8,128)(2,1)}, u32[]{:S(2)}) %copy-start.1) | copy-done | bytes 131096
  3.4 0.0 copy-start.2
  3.4 0.7 %copy-done.2 = s32[4]{0:T(128)S(1)} copy-done((s32[4]{0:T(128)S(1)}, s32[4]{0:T(128)}, u32[]{:S(2)}) %copy-start.2) | copy-done | bytes 40
  4.1 40.1 %shard_map.46 = f32[4,16,128]{2,1,0:T(8,128)S(1)} custom-call(s32[4]{0:T(128)S(1)} %copy-done.2, s32[4,2]{1,0:T(4,128)S(1)} %copy.5.cmap_ref, bf16[4,16,1024]{2,1,0:T(8,128)(2,1)S(1)} %bitcast.5, bf16[5,2,4,2,32,512]{5,4,3,2,1,0:T(8,128)(2,1)S(1)} %bitcast.4), custom_call_target="tpu_custom_call" | custom-call | tf_op jit(solution)/shard_map/pallas_call | solution.py:180
  44.2 0.1 reshape.10
  44.3 0.6 %copy.6 = f32[4,64,2,16]{1,3,2,0:T(8,128)} copy(f32[4,64,2,16]{1,2,3,0:T(2,128)S(1)} %bitcast.6) | data formatting | bytes 65536 | tf_op jit(solution)/shard_map/transpose | solution.py:222
Async XLA Ops:
  0.8 1.7 %copy-start = (bf16[1,5,512,512]{3,2,1,0:T(8,128)(2,1)S(1)}, bf16[1,5,512,512]{3,2,1,0:T(8,128)(2,1)}, u32[]{:S(2)}) copy-start(bf16[1,5,512,512]{3,2,1,0:T(8,128)(2,1)} %param.5) | copy-start | bytes 7864324
  2.5 0.9 %copy-start.1 = (bf16[1,4,16,1024]{3,2,1,0:T(8,128)(2,1)S(1)}, bf16[1,4,16,1024]{3,2,1,0:T(8,128)(2,1)}, u32[]{:S(2)}) copy-start(bf16[1,4,16,1024]{3,2,1,0:T(8,128)(2,1)} %param.4) | copy-start | bytes 393220
  3.4 0.7 %copy-start.2 = (s32[4]{0:T(128)S(1)}, s32[4]{0:T(128)}, u32[]{:S(2)}) copy-start(s32[4]{0:T(128)} %owners_ref.1) | copy-start | bytes 52

commit v2 on v1

v2 whole, which is shorter than its diff:
```python
import functools

import jax
import jax.numpy as jnp
from jax import lax
from jax.experimental import pallas as pl
from jax.experimental.pallas import tpu as pltpu
from jax.sharding import PartitionSpec as P

MESH = pl.DeviceIdType.MESH
NZ, NY, NC = 4, 4, 2
NG = 8
B = 512


def kernel(
    owners_ref, cmap_ref, grads_ref, bank_ref, out_ref,
    rx1, part_buf, rx2, s_buf, l_buf, r_all, r_buf, r_tx, u_buf, rx3, p_buf, rx4,
    owners_buf, cmap_buf, loc_sem, s1, r1, sz, rz, sy, ry, sc, rc, sf, rf, s3, r3, s4, r4,
):
    g = lax.axis_index("grp")
    w = lax.axis_index("wk")
    z, y, c = w // 8, (w // 2) % 4, w % 2
    h, x = g // 4, g % 4
    l, j = x, h

    def wk(zz, yy, cc):
        return zz * 8 + yy * 2 + cc

    peer = (g, wk(z, y, 1 - c))

    def local(src, dst, sem):
        return pltpu.make_async_copy(src, dst, sem)

    begun, landed = [], []

    def send(src, dst, ssem, rsem, dev):
        copy = pltpu.make_async_remote_copy(
            src_ref=src, dst_ref=dst, send_sem=ssem, recv_sem=rsem,
            device_id=dev, device_id_type=MESH,
        )
        copy.start()
        begun.append(copy)
        return copy

    def arrive(copy):
        copy.wait_recv()
        landed.append(copy)

    def grp(hh, xx):
        return hh * 4 + xx

    cp_g = local(grads_ref.at[x], rx1.at[0], loc_sem.at[0])
    cp_l = local(bank_ref.at[0], l_buf.at[c], loc_sem.at[1])
    cp_r = local(bank_ref.at[pl.ds(1, 4)], r_all, loc_sem.at[2])
    cp_o = local(owners_ref, owners_buf, loc_sem.at[3])
    cp_m = local(cmap_ref, cmap_buf, loc_sem.at[4])
    cp_g.start()
    cp_o.start()
    cp_m.start()
    cp_l.start()
    cp_r.start()

    barrier = pltpu.get_barrier_semaphore()
    mates = [(grp(h, (x + off) % 4), w) for off in range(1, 4)]
    mates += [(grp((h + dh) % 2, x), wk((z + dz) % NZ, y, c)) for dh in range(2) for dz in range(NZ) if dh or dz]
    mates += [(g, wk(z, (y + off) % NY, c)) for off in range(1, NY)]
    mates.append(peer)
    for mate in mates:
        pl.semaphore_signal(barrier, inc=1, device_id=mate, device_id_type=MESH)
    pl.semaphore_wait(barrier, len(mates))

    first = []
    for off in (2, 1, 3):
        x2 = (x + off) % 4
        first.append(send(grads_ref.at[x2], rx1.at[off], s1.at[off], r1.at[off], (grp(h, x2), w)))

    cp_l.wait()
    f_l = send(l_buf.at[c], l_buf.at[c], sf.at[0], rf.at[0], peer)
    cp_r.wait()
    cp_o.wait()
    cp_m.wait()
    block = cmap_buf[j, l]
    for zz in range(2):
        for yy in range(NY):
            r_tx[yy, zz] = r_all[block, zz, yy, 1 - c]
    f_r = send(r_tx, r_buf.at[c], sf.at[1], rf.at[1], peer)
    for zz in range(2):
        for yy in range(NY):
            r_buf[c, yy, zz] = r_all[block, zz, yy, c]

    cp_g.wait()
    for cp in first:
        arrive(cp)
    total = rx1[0].astype(jnp.float32)
    for k in range(1, 4):
        total += rx1[k].astype(jnp.float32)
    total = total.astype(jnp.bfloat16)
    for jj in range(2):
        part_buf[jj] = total[:, jj * B:(jj + 1) * B]
    rx2[h, z] = part_buf[h]

    zs = {}
    for dz in (0, 1, 3, 2):
        for dh in (1, 0):
            if dh or dz:
                h2 = (h + dh) % 2
                zs[dz, dh] = send(part_buf.at[h2], rx2.at[h, z], sz.at[dz, dh], rz.at[dz, dh],
                                  (grp(h2, x), wk((z + dz) % NZ, y, c)))
    ys, cs = [], []

    def pass_on(k, off):
        part = s_buf.at[(z - k + NZ) % NZ, (y - off + NY) % NY, c]
        cs.append(send(part, part, sc.at[k, off], rc.at[k, off], peer))

    for k in (2, 1, 3, 0):
        if k:
            arrive(zs[k, 0])
        arrive(zs[k, 1])
        zz = (z - k + NZ) % NZ
        both = rx2[0, zz].astype(jnp.float32) + rx2[1, zz].astype(jnp.float32)
        s_buf[zz, y, c] = both.astype(jnp.bfloat16)
        part = s_buf.at[zz, y, c]
        for off in (2, 1, 3):
            ys.append((k, off, send(part, part, sy.at[k, off - 1], ry.at[k, off - 1], (g, wk(z, (y + off) % NY, c)))))
        pass_on(k, 0)
    for k, off, cp in ys:
        arrive(cp)
        pass_on(k, off)
    arrive(f_l)
    arrive(f_r)
    for cp in cs:
        arrive(cp)

    owner = owners_buf[l]
    o_y, o_c = (owner // 2) % 4, owner % 2
    right = r_buf[o_c].reshape(2 * NY * 32, B)
    summed = s_buf[...].reshape(B, B)
    mixed = lax.dot_general(right, summed, (((1,), (1,)), ((), ())), preferred_element_type=jnp.float32)
    update = jnp.dot(mixed.astype(jnp.bfloat16), l_buf[o_c].reshape(B, B), preferred_element_type=jnp.float32)
    u_buf[...] = update.astype(jnp.bfloat16).reshape(NY, 2, 32, B)

    us = []
    for off in range(1, NY):
        y2 = (y + off) % NY
        us.append(send(u_buf.at[y2], rx3.at[y], s3.at[off - 1], r3.at[off - 1], (g, wk(z, y2, c))))
    rx3[y] = u_buf[y]
    for cp in us:
        arrive(cp)

    low = lax.broadcasted_iota(jnp.int32, (16, 128), 1) < 64
    for zz in range(2):
        for b in range(4):
            top = rx3[o_y, zz, pl.ds(0, 16), pl.ds(128 * b, 128)].astype(jnp.float32)
            bot = rx3[o_y, zz, pl.ds(16, 16), pl.ds(128 * b, 128)].astype(jnp.float32)
            p_buf[zz, 2 * b] = jnp.where(low, top, pltpu.roll(bot, 64, 1)).astype(jnp.bfloat16)
            p_buf[zz, 2 * b + 1] = jnp.where(low, pltpu.roll(top, 64, 1), bot).astype(jnp.bfloat16)
    kept = []
    for dh, dx in ((1, 2), (1, 1), (1, 3), (1, 0), (0, 2), (0, 1), (0, 3), (0, 0)):
        g2 = grp((h + dh) % 2, (x + dx) % 4)
        for zz in range(2):
            z2 = 2 * j + zz
            k = 4 * dh + dx
            dev = (g2, wk(z2, y, c))
            if k:
                send(p_buf.at[zz, g2], rx4.at[l, z], s4.at[zz, k], r4.at[l, z], dev)
            else:
                own = local(p_buf.at[zz, g2], rx4.at[l, z], r4.at[l, z])
                far = pltpu.make_async_remote_copy(
                    src_ref=p_buf.at[zz, g2], dst_ref=rx4.at[l, z], send_sem=s4.at[zz, k], recv_sem=r4.at[l, z],
                    device_id=dev, device_id_type=MESH)
                pl.when(z2 == z)(own.start)
                pl.when(z2 != z)(far.start)
                kept.append((z2, far))
    for layer in range(4):
        for zz in range(NZ):
            local(p_buf.at[0, 0], rx4.at[layer, zz], r4.at[layer, zz]).wait()
    for z2, far in kept:
        pl.when(z2 != z)(far.wait_send)
    for cp in begun:
        cp.wait_send()
    for layer in range(4):
        tile = rx4[layer, owners_buf[layer] // 8].astype(jnp.float32)
        out_ref[layer, pl.ds(0, 16)] = tile[:, :64]
        out_ref[layer, pl.ds(16, 16)] = pltpu.roll(tile, 64, 1)[:, :64]


def solution(mesh):
    def step(grads, bank, owners, cmap):
        packed = pl.pallas_call(
            kernel,
            out_shape=jax.ShapeDtypeStruct((4, 32, 64), jnp.float32),
            in_specs=[
                pl.BlockSpec(memory_space=pl.ANY),
                pl.BlockSpec(memory_space=pl.ANY),
                pl.BlockSpec(memory_space=pl.ANY),
                pl.BlockSpec(memory_space=pl.ANY),
            ],
            out_specs=pl.BlockSpec(memory_space=pltpu.VMEM),
            scratch_shapes=[
                pltpu.VMEM((4, 16, 2 * B), jnp.bfloat16),
                pltpu.VMEM((2, 16, B), jnp.bfloat16),
                pltpu.VMEM((2, NZ, 16, B), jnp.bfloat16),
                pltpu.VMEM((NZ, NY, NC, 16, B), jnp.bfloat16),
                pltpu.VMEM((NC, 2, NY, NC, 32, B), jnp.bfloat16),
                pltpu.VMEM((4, 2, NY, NC, 32, B), jnp.bfloat16),
                pltpu.VMEM((NC, NY, 2, 32, B), jnp.bfloat16),
                pltpu.VMEM((NY, 2, 32, B), jnp.bfloat16),
                pltpu.VMEM((NY, 2, 32, B), jnp.bfloat16),
                pltpu.VMEM((NY, 2, 32, B), jnp.bfloat16),
                pltpu.VMEM((2, NG, 16, 128), jnp.bfloat16),
                pltpu.VMEM((4, NZ, 16, 128), jnp.bfloat16),
                pltpu.SMEM((4,), jnp.int32),
                pltpu.SMEM((2, 4), jnp.int32),
                pltpu.SemaphoreType.DMA((5,)),
                pltpu.SemaphoreType.DMA((4,)),
                pltpu.SemaphoreType.DMA((4,)),
                pltpu.SemaphoreType.DMA((NZ, 2)),
                pltpu.SemaphoreType.DMA((NZ, 2)),
                pltpu.SemaphoreType.DMA((NZ, NY - 1)),
                pltpu.SemaphoreType.DMA((NZ, NY - 1)),
                pltpu.SemaphoreType.DMA((NZ, NY)),
                pltpu.SemaphoreType.DMA((NZ, NY)),
                pltpu.SemaphoreType.DMA((2,)),
                pltpu.SemaphoreType.DMA((2,)),
                pltpu.SemaphoreType.DMA((NY - 1,)),
                pltpu.SemaphoreType.DMA((NY - 1,)),
                pltpu.SemaphoreType.DMA((2, NG)),
                pltpu.SemaphoreType.DMA((4, NZ)),
            ],
            compiler_params=pltpu.CompilerParams(
                collective_id=0, has_side_effects=True, vmem_limit_bytes=56 * 1024 * 1024
            ),
        )(owners, cmap.T, grads[0], bank.reshape(5, 2, NY, NC, 32, B))
        return packed.transpose(0, 2, 1)

    return jax.shard_map(
        step, mesh=mesh,
        in_specs=(P("grp", None, "wk", None), P("wk", None, None, None), P(), P()),
        out_specs=P(None, "grp", "wk"), check_vma=False,
    )
```

time: 45 us -> 37 us (0.82)
  Pallas kernels: 40.1 us -> 35.3 us
  local copies, waits for them, and re-layouts: 4.79 us -> 1.47 us
    pallas_call x1, Pallas kernels: 40.1 us -> 35.3 us  [step(): pl.pallas_call(kernel, out_shape=jax.ShapeDtypeStruct((4, 32, 64), jnp.fl...]
    unnamed x7 -> x1, local copies, waits for them, and re-layouts: 4.06 us -> 1.47 us
    transpose x1 -> x0, local copies, waits for them, and re-layouts: 0.63 us -> none  [step(): return packed.transpose(0, 3, 2, 1).reshape(4, 64, 32)]
where the time goes in v2:
time: 37 us; the launch traced here: 36.8 us
  Pallas kernels  35.3 us (95%)
  local copies, waits for them, and re-layouts  1.47 us (4%)
    pallas_call x1, Pallas kernels, step(): pl.pallas_call(kernel, out_shape=jax.ShapeDtypeStruct((4, 32, 64), jnp.fl...  35.3 us
    unnamed x1, local copies, waits for them, and re-layouts  1.47 us

profile of v2, /device:TPU:1, one launch (start us, length us, event | category | flops | bytes accessed | tf_op | source)
XLA Modules:
  0.0 36.8 jit_solution(11783531370722232204)
XLA Ops:
  0.0 35.3 %shard_map.46 = f32[4,32,64]{2,1,0:T(8,128)} custom-call(s32[4]{0:T(128)} %owners_ref.1, s32[2,4]{1,0:T(2,128)} %bitcast.7, bf16[4,16,1024]{2,1,0:T(8,128)(2,1)} %bitcast.6, bf16[5,2,4,2,32,512]{5,4,3,2,1,0:T(8,128)(2,1)} %bitcast.4), custom_call_target="tpu_custom_call" | custom-call | tf_op jit(solution)/shard_map/pallas_call | solution.py:190
  35.4 1.5 %copy.6 = f32[4,64,32]{1,2,0:T(8,128)} copy(f32[4,64,32]{1,2,0:T(8,128)} %bitcast.5) | data formatting | bytes 65536
